TPU v7x, 128 devices: a whole 4x4x4 slice. The times are simulated.
128 devices in a mesh: stream: 8 (over x, core), depth: 16 (over y, z).
Axes of the slice: x: 4, y: 4, z: 4, core: 2. Of those that a mesh axis runs over, the one named last changes fastest.
Arguments:
- velocity: bfloat16 [3, 512, 768, 128], P(None, 'stream', 'depth'), may hold values from -6 to 6
- diffusion: bfloat16 [512, 768, 128], P('stream', 'depth'), may hold values from 0.0099487305 to 0.05493164
- advection: bfloat16 [512, 768, 128], P('stream', 'depth'), may hold values from 0.049804688 to 0.29882812
- normals: bfloat16 [8, 16, 3, 128, 128], P('stream', 'depth'), may hold values from -3 to 3
- tile_cell: int32 [8, 16, 128], P('stream', 'depth'), may hold values from 0 to 3071
- tile_class: int32 [8, 16, 128], P('stream', 'depth'), may hold values from 0 to 7
- tile_leaf: int32 [8, 16, 128], P('stream', 'depth'), may hold values from 0 to 63
- tile_owner: int32 [8, 16, 128, 1], P('stream', 'depth'), may hold values from 0 to 127; in each aligned block of 128 rows (0 to 127, 128 to 255, ..., all dimensions but the last counted through in order) at most 2 rows name the same one
- source_expansion: bfloat16 [8, 128, 289], replicated, may hold values from -0.5 to 0.5
- translation: float32 [8, 289, 289], replicated, may hold values from -0.125 to 0.125
- leaf_octant: int32 [8, 16, 8, 8], P('stream', 'depth'), may hold values from 0 to 7, each once within a row
- node_octant: int32 [8, 16, 8], P('stream', 'depth'), may hold values from 0 to 7, each once within a row
- subtree_octant: int32 [8, 2, 8], P('stream'), may hold values from 0 to 7, each once within a row
- cluster_octant: int32 [2, 8], replicated, may hold values from 0 to 7, each once within a row
- root_octant: int32 [8], replicated, may hold values from 0 to 7, each once
Outputs:
- flow: float32 [3, 512, 768, 128], P(None, 'stream', 'depth')
- leaf_multipoles: float32 [8, 16, 64, 289], P('stream', 'depth')
- upper_multipoles: float32 [19, 289], replicated
Inputs may be any that keep to these rules, and one draw needn't show every extreme that they name: `tile_owner`: among the tiles of one device no owner is named more than 2 times, a bound that some block reaches. Owners are numbered with the stream index slowest. `tile_cell`: cells of a device's block are numbered with the depth index fastest. `leaf_octant`: each row of eight holds every octant once. `node_octant`: each row of eight holds every octant once. `subtree_octant`: each row of eight holds every octant once. `cluster_octant`: each row of eight holds every octant once. `root_octant`: holds every octant once.
All inputs are finite; a program needn't handle non-finite values.
Results may differ from a plain program's by a relative error of at most 0.0029.
Values may be sent and summed in bfloat16 or wider, within the bound.
A program may use at most 192 MiB of HBM per device.

v0:
```python
import functools

import jax
import jax.numpy as jnp
from jax import lax
from jax.experimental import pallas as pl
from jax.experimental.pallas import tpu as pltpu
from jax.sharding import PartitionSpec as P

MESH = pl.DeviceIdType.MESH
F32, BF16, I32 = jnp.float32, jnp.bfloat16, jnp.int32
SX, SD, SPAN, SWEEPS, TILES, COEF, LEAVES = 64, 48, 128, 4, 128, 289, 64
NS, ND = 8, 16
SLAB, LEAD = 64, 8
KP = 384
KR = 304
SLOTS = 2 * NS * ND


def split(value):
    high = value.astype(BF16).astype(F32)
    return high, value - high


def dot(a, b):
    return jnp.dot(a, b, preferred_element_type=F32)


def dot_nt(a, b):
    return lax.dot_general(a, b, (((1,), (1,)), ((), ())), preferred_element_type=F32)


def iota(shape, dim):
    return lax.broadcasted_iota(I32, shape, dim)


def kernel(
    cell, loct, noct, soct, coct, roct,
    owner, cls, leaf,
    vel, dif, adv, nrm, exp, tr,
    flow, leaves, upper,
    velv, difv, advv, nrmv, expv, trv, tv, ef, et, wh, wl, qa, qb, al, ka, be,
    pmat, perm, gg, picked, order,
    xs, xr, ds, dr, m1s, m1r, m2s, m2r, a1s, a1r, a2s, a2r, e1s, e1r, e2s, e2r,
    lsem, hss, hrs, m1ss, m1rs, m2ss, m2rs, a1ss, a1rs, a2ss, a2rs, e1ss, e1rs, e2ss, e2rs,
):
    i, j = lax.axis_index("stream"), lax.axis_index("depth")

    loads = [
        pltpu.make_async_copy(s, d, lsem.at[n])
        for n, (s, d) in enumerate(
            (
                (vel, velv),
                (dif, difv),
                (adv, advv),
                (nrm, nrmv),
                (exp, expv),
                (tr.at[:, pl.ds(0, SPAN)], tv.at[0, pl.ds(0, 8 * COEF), :]),
                (tr.at[:, pl.ds(SPAN, SPAN)], tv.at[1, pl.ds(0, 8 * COEF), :]),
                (tr.at[:, pl.ds(2 * SPAN, COEF - 2 * SPAN)], trv),
            )
        )
    ]
    for copy in loads:
        copy.start()

    barrier = pltpu.get_barrier_semaphore()
    for r in range(1, ND):
        pl.semaphore_signal(barrier, inc=1, device_id=(i, lax.rem(j + r, ND)), device_id_type=MESH)
    for r in range(1, NS):
        pl.semaphore_signal(barrier, inc=1, device_id=(lax.rem(i + r, NS), j), device_id_type=MESH)

    def along_depth(src, dst, ss, rs):
        return [
            pltpu.make_async_remote_copy(
                src_ref=src(lax.rem(j + r, ND)), dst_ref=dst.at[j], send_sem=ss.at[r], recv_sem=rs.at[r],
                device_id=(i, lax.rem(j + r, ND)), device_id_type=MESH,
            )
            for r in range(1, ND)
        ]

    def along_stream(src, dst, ss, rs):
        return [
            pltpu.make_async_remote_copy(
                src_ref=src(lax.rem(i + r, NS)), dst_ref=dst.at[i], send_sem=ss.at[r], recv_sem=rs.at[r],
                device_id=(lax.rem(i + r, NS), j), device_id_type=MESH,
            )
            for r in range(1, NS)
        ]

    def start(copies):
        for copy in copies:
            copy.start()

    def arrive(copies):
        for copy in copies:
            copy.wait_recv()

    def sent(copies):
        for copy in copies:
            copy.wait_send()

    def halo(n):
        xlow = velv.at[:, 0] if n == 0 else xs.at[n, 0]
        xhigh = velv.at[:, SX - 1] if n == 0 else xs.at[n, 1]

        def copy(src, dst, which, device):
            return pltpu.make_async_remote_copy(
                src_ref=src, dst_ref=dst, send_sem=hss.at[n, which], recv_sem=hrs.at[n, which],
                device_id=device, device_id_type=MESH,
            )

        return (
            (i < NS - 1, i > 0, copy(xhigh, xr.at[n, 0], 0, (lax.rem(i + 1, NS), j))),
            (i > 0, i < NS - 1, copy(xlow, xr.at[n, 1], 1, (lax.rem(i + NS - 1, NS), j))),
            (j < ND - 1, j > 0, copy(ds.at[n, 1], dr.at[n, 0], 2, (i, lax.rem(j + 1, ND)))),
            (j > 0, j < ND - 1, copy(ds.at[n, 0], dr.at[n, 1], 3, (i, lax.rem(j + ND - 1, ND)))),
        )

    def halo_start(n):
        for send, _, copy in halo(n):
            pl.when(send)(copy.start)

    def halo_arrive(n):
        for _, receive, copy in halo(n):
            pl.when(receive)(copy.wait_recv)

    def halo_sent(n):
        for send, _, copy in halo(n):
            pl.when(send)(copy.wait_send)

    for edge, ref, side in ((i == 0, xr, 0), (i == NS - 1, xr, 1), (j == 0, dr, 0), (j == ND - 1, dr, 1)):

        @pl.when(edge)
        def _(ref=ref, side=side):
            for n in range(SWEEPS):
                ref[n, side] = jnp.zeros(ref.shape[2:], BF16)

    zero8 = jnp.zeros((8, SPAN), F32)
    for q in (qa, qb):
        for k in range(3):
            for x in (0, SX + 1):
                q[k, pl.ds(x * SLAB, SLAB), :] = jnp.zeros((SLAB, SPAN), F32)

    def clear(x, carry):
        for q in (qa, qb):
            for k in range(3):
                q[k, pl.ds(pl.multiple_of(x * SLAB, 8), 8), :] = zero8
                q[k, pl.ds(pl.multiple_of(x * SLAB + LEAD + SD, 8), 8), :] = zero8
        return carry

    lax.fori_loop(1, SX + 1, clear, 0)

    own = owner[...]
    across = jnp.broadcast_to(own.astype(F32), (TILES, TILES))
    down = jnp.transpose(across)
    before = iota((TILES, TILES), 0) < iota((TILES, TILES), 1)
    rank = jnp.sum(jnp.where((across == down) & before, 1.0, 0.0), axis=0, keepdims=True).astype(I32)
    slot = (own & (ND - 1)) * (2 * NS) + (own >> 4) * 2 + rank
    pmat[...] = jnp.where(iota((SLOTS, TILES), 0) == slot, 1.0, 0.0).astype(BF16)
    feature = iota((SPAN, TILES), 0)
    meta = jnp.where((feature == leaf[...]) | (feature == cls[...] + LEAVES), 1.0, 0.0).astype(BF16)
    m1s[...] = dot_nt(pmat[...], meta).astype(BF16).reshape(ND, 2 * NS, SPAN)
    out = iota((SLOTS, SLOTS), 0)
    source = ((out >> 1) & (ND - 1)) * (2 * NS) + (out >> 5) * 2 + (out & 1)
    perm[...] = jnp.where(iota((SLOTS, SLOTS), 1) == source, 1.0, 0.0).astype(BF16)

    for copy in loads[:3]:
        copy.wait()

    def widen(x, carry):
        at = pl.multiple_of((x + 1) * SLAB + LEAD, 8)
        for k in range(3):
            qa[k, pl.ds(at, SD), :] = velv[k, x].astype(F32)
        kappa = difv[x].astype(F32)
        speed = advv[x].astype(F32)
        rows = pl.ds(pl.multiple_of(x * SD, 8), SD)
        ka[rows, :] = kappa
        be[rows, :] = kappa + speed
        al[rows, :] = 1.0 - 6.0 * kappa - speed
        return carry

    lax.fori_loop(0, SX, widen, 0)
    low = pl.ds(SLAB + LEAD, SX, stride=SLAB)
    high = pl.ds(SLAB + LEAD + SD - 1, SX, stride=SLAB)
    for k in range(3):
        ds[0, 0, k] = qa[k, low, :].astype(BF16)
        ds[0, 1, k] = qa[k, high, :].astype(BF16)

    pl.semaphore_wait(barrier, ND - 1 + NS - 1)
    halo_start(0)
    meta1 = along_depth(lambda p: m1s.at[p], m1r, m1ss, m1rs)
    start(meta1)
    m1r[j] = m1s[j]

    def sweep(src, dst, pitch, lead):
        def step(x, carry):
            rows = pl.ds(pl.multiple_of(x * SD, 8), SD)
            kappa, beta, alpha = ka[rows, :], be[rows, :], al[rows, :]
            at = (x + 1) * SLAB + LEAD
            for k in range(3):
                view = src.at[k]
                c = view[pl.ds(pl.multiple_of(at, 8), SD), :]
                f = view[pl.ds(pl.multiple_of(at + SLAB, 8), SD), :]
                b = view[pl.ds(pl.multiple_of(at - SLAB, 8), SD), :]
                up = view[pl.ds(at + 1, SD), :]
                down = view[pl.ds(at - 1, SD), :]
                total = f + (up + down) + (pltpu.roll(c, 1, 1) + pltpu.roll(c, SPAN - 1, 1))
                dst[k, pl.ds(pl.multiple_of(x * pitch + lead, 8), SD), :] = alpha * c + kappa * total + beta * b
            return carry

        lax.fori_loop(0, SX, step, 0)

    def faces(n, dst, pitch, lead):
        first = pl.ds(lead, SD)
        last = pl.ds((SX - 1) * pitch + lead, SD)
        low = pl.ds(lead, SX, stride=pitch)
        high = pl.ds(lead + SD - 1, SX, stride=pitch)
        klow = ka[pl.ds(0, SX, stride=SD), :]
        khigh = ka[pl.ds(SD - 1, SX, stride=SD), :]
        for k in range(3):
            dst[k, first, :] = dst[k, first, :] + be[pl.ds(0, SD), :] * xr[n, 0, k].astype(F32)
            dst[k, last, :] = dst[k, last, :] + ka[pl.ds((SX - 1) * SD, SD), :] * xr[n, 1, k].astype(F32)
            ql = dst[k, low, :] + klow * dr[n, 0, k].astype(F32)
            qh = dst[k, high, :] + khigh * dr[n, 1, k].astype(F32)
            dst[k, low, :] = ql
            dst[k, high, :] = qh
            if n + 1 < SWEEPS:
                ds[n + 1, 0, k] = ql.astype(BF16)
                ds[n + 1, 1, k] = qh.astype(BF16)
                xs[n + 1, 0, k] = dst[k, first, :].astype(BF16)
                xs[n + 1, 1, k] = dst[k, last, :].astype(BF16)
        if n + 1 < SWEEPS:
            halo_start(n + 1)

    sweep(qa, qb, SLAB, SLAB + LEAD)
    for copy in loads[5:]:
        copy.wait()
    for w in (wh, wl):
        for o in range(8):
            w[o, pl.ds(KR, KP - KR), :] = jnp.zeros((KP - KR, KP), BF16)
    tv[:, pl.ds(8 * COEF, 8 * (KR - COEF)), :] = jnp.zeros((3, 8 * (KR - COEF), SPAN), F32)
    tv[2, pl.ds(0, 8 * COEF), :] = jnp.concatenate(
        [trv[...], jnp.zeros((8 * COEF, KP - COEF), F32)], axis=1
    )

    def halve(b, carry):
        for o in range(8):
            rows = pl.ds(b * 128 + o, 16, stride=8)
            to = pl.ds(pl.multiple_of(b * 16, 16), 16)
            for n in range(3):
                lanes = pl.ds(n * SPAN, SPAN)
                h, l = split(tv[n, rows, :])
                wh[o, to, lanes] = h.astype(BF16)
                wl[o, to, lanes] = l.astype(BF16)
        return carry

    lax.fori_loop(0, KR // 16, halve, 0)
    halo_arrive(0)
    faces(0, qb, SLAB, SLAB + LEAD)

    sweep(qb, qa, SLAB, SLAB + LEAD)
    arrive(meta1)
    m2s[...] = dot(perm[...], m1r[...].reshape(SLOTS, SPAN)).astype(BF16).reshape(NS, 2 * ND, SPAN)
    meta2 = along_stream(lambda p: m2s.at[p], m2r, m2ss, m2rs)
    start(meta2)
    m2r[i] = m2s[i]
    loads[4].wait()
    et[pl.ds(KR, KP - KR), :] = jnp.zeros((KP - KR, 8 * SPAN), BF16)
    ef[pl.ds(0, 8 * COEF), :] = expv[...].astype(F32)
    ef[pl.ds(8 * COEF, 8 * (KR - COEF)), :] = jnp.zeros((8 * (KR - COEF), SPAN), F32)

    def classes(b, carry):
        for c in range(8):
            value = ef[pl.ds(b * 128 + c, 16, stride=8), :]
            et[pl.ds(pl.multiple_of(b * 16, 16), 16), pl.ds(c * SPAN, SPAN)] = value.astype(BF16)
        return carry

    lax.fori_loop(0, KR // 16, classes, 0)
    halo_arrive(1)
    faces(1, qa, SLAB, SLAB + LEAD)

    sweep(qa, qb, SLAB, SLAB + LEAD)
    arrive(meta2)
    lane = iota((1, SPAN), 1)
    octant = jnp.full((1, SPAN), -1, I32)
    for l in range(LEAVES):
        octant = jnp.where(lane == l, loct[l // 8, l % 8], octant)
    row = iota((SPAN, SPAN), 0)
    ordered = jnp.where((row & 7) == (lane >> 3), jnp.where((row >> 3) == octant, 1.0, 0.0), 0.0)
    order[...] = jnp.transpose(ordered).astype(BF16)
    arrived = m2r[...].reshape(SLOTS, SPAN)
    leaf_of = dot_nt(ordered[:LEAVES].astype(BF16), arrived)
    pick = jnp.where(iota((8, SPAN), 1) == iota((8, SPAN), 0) + LEAVES, 1.0, 0.0).astype(BF16)
    class_of = dot_nt(pick, arrived)
    for c in range(8):
        gg[pl.ds(c * LEAVES, LEAVES), :] = (leaf_of * class_of[c : c + 1, :]).astype(BF16)
    halo_arrive(2)
    faces(2, qb, SLAB, SLAB + LEAD)

    sweep(qb, flow, SD, 0)
    halo_arrive(3)
    faces(3, flow, SD, 0)

    loads[3].wait()

    def sample(t, carry):
        for k in range(3):
            picked[k, t] = flow[k, cell[0, t]]
        return carry

    lax.fori_loop(0, TILES, sample, 0, unroll=8)
    strength = nrmv[0].astype(F32) * picked[0]
    for k in (1, 2):
        strength = strength + nrmv[k].astype(F32) * picked[k]
    a1s[...] = dot(pmat[...], strength.astype(BF16)).astype(BF16).reshape(ND, 2 * NS, SPAN)
    data1 = along_depth(lambda p: a1s.at[p], a1r, a1ss, a1rs)
    start(data1)
    a1r[j] = a1s[j]
    arrive(data1)
    a2s[...] = dot(perm[...], a1r[...].reshape(SLOTS, SPAN)).astype(BF16).reshape(NS, 2 * ND, SPAN)
    data2 = along_stream(lambda p: a2s.at[p], a2r, a2ss, a2rs)
    start(data2)
    a2r[i] = a2s[i]
    arrive(data2)

    sums = dot(gg[...], a2r[...].reshape(SLOTS, SPAN))
    blocks = []
    for c in range(8):
        h, l = split(sums[c * LEAVES : (c + 1) * LEAVES])
        blocks.append(jnp.concatenate([h, l], axis=0).astype(BF16))
    both = dot_nt(jnp.concatenate(blocks, axis=1), et[...])
    ordered_leaves = both[:LEAVES] + both[LEAVES:]

    h, l = split(ordered_leaves)
    lhs = jnp.concatenate(
        [jnp.concatenate([h[8 * o : 8 * o + 8], l[8 * o : 8 * o + 8]], axis=0).astype(BF16) for o in range(8)], axis=1
    )
    product = dot(lhs, wh[...].reshape(8 * KP, KP)) + dot(lhs, wl[...].reshape(8 * KP, KP))
    h, l = split(product[:8] + product[8:])
    node = iota((16, KP), 0) & 7
    octant = jnp.full((16, KP), -1, I32)
    for p in range(8):
        octant = jnp.where(node == p, noct[0, p], octant)
    stacked = jnp.concatenate([h, l], axis=0)
    lhs = jnp.concatenate([jnp.where(octant == o, stacked, 0.0).astype(BF16) for o in range(8)], axis=1)
    subtree = jnp.sum(dot(lhs, wh[...].reshape(8 * KP, KP)) + dot(lhs, wl[...].reshape(8 * KP, KP)), axis=0, keepdims=True)

    group, member = j >> 3, j & 7

    def lift(vector, which):
        h, l = split(vector)
        place = iota((16, KP), 0)
        rows = jnp.where(place == 0, h, jnp.where(place == 1, l, 0.0)).astype(BF16)
        return jnp.sum(dot(rows, wh[which]) + dot(rows, wl[which]), axis=0, keepdims=True)

    in_cluster = lift(subtree, soct[group, member])
    in_half = lift(in_cluster, coct[group, i])
    in_root = lift(in_half, roct[0, group])
    e1s[...] = jnp.concatenate([in_cluster, in_half, in_root], axis=1)
    terms = along_depth(lambda p: e1s, e1r, e1ss, e1rs)
    start(terms)
    e1r[j] = e1s[...]

    h, rest = split(ordered_leaves)
    m, l = split(rest)
    turn = order[:LEAVES, :LEAVES]
    leaves[...] = (dot(turn, h.astype(BF16)) + dot(turn, m.astype(BF16)) + dot(turn, l.astype(BF16)))[:, :COEF]

    arrive(terms)
    halves = []
    for g in range(2):
        total = e1r[8 * g]
        for m in range(1, 8):
            total = total + e1r[8 * g + m]
        halves.append(total)
    e2s[...] = jnp.concatenate(
        [
            halves[0][:, :KP],
            halves[1][:, :KP],
            halves[0][:, KP : 2 * KP],
            halves[1][:, KP : 2 * KP],
            halves[0][:, 2 * KP :] + halves[1][:, 2 * KP :],
        ],
        axis=1,
    )
    rows = along_stream(lambda p: e2s, e2r, e2ss, e2rs)
    start(rows)
    e2r[i] = e2s[...]
    arrive(rows)
    total = e2r[0][:, 2 * KP :]
    for s in range(1, NS):
        total = total + e2r[s][:, 2 * KP :]
    for s in range(NS):
        value = e2r[s]
        for g in range(2):
            upper[pl.ds(2 * s + g, 1), :] = value[:, g * KP : g * KP + COEF]
    for n in range(3):
        upper[pl.ds(2 * NS + n, 1), :] = total[:, n * KP : n * KP + COEF]

    for n in range(SWEEPS):
        halo_sent(n)
    for copies in (meta1, meta2, data1, data2, terms, rows):
        sent(copies)


def per_device(
    velocity, diffusion, advection, normals, tile_cell, tile_class, tile_leaf, tile_owner,
    source_expansion, translation, leaf_octant, node_octant, subtree_octant, cluster_octant, root_octant,
):
    smem = pl.BlockSpec(memory_space=pltpu.SMEM)
    vmem = pl.BlockSpec(memory_space=pltpu.VMEM)
    hbm = pl.BlockSpec(memory_space=pl.ANY)
    dma = pltpu.SemaphoreType.DMA
    rows = (SX + 2) * SLAB
    flow, leaves, upper = pl.pallas_call(
        kernel,
        out_shape=(
            jax.ShapeDtypeStruct((3, SX * SD, SPAN), F32),
            jax.ShapeDtypeStruct((LEAVES, COEF), F32),
            jax.ShapeDtypeStruct((2 * NS + 3, COEF), F32),
        ),
        in_specs=[smem] * 6 + [vmem] * 3 + [hbm] * 6,
        out_specs=(vmem, vmem, vmem),
        scratch_shapes=[
            pltpu.VMEM((3, SX, SD, SPAN), BF16),
            pltpu.VMEM((SX, SD, SPAN), BF16),
            pltpu.VMEM((SX, SD, SPAN), BF16),
            pltpu.VMEM((3, TILES, SPAN), BF16),
            pltpu.VMEM((8 * COEF, SPAN), BF16),
            pltpu.VMEM((8 * COEF, COEF - 2 * SPAN), F32),
            pltpu.VMEM((3, 8 * KR, SPAN), F32),
            pltpu.VMEM((8 * KR, SPAN), F32),
            pltpu.VMEM((KP, 8 * SPAN), BF16),
            pltpu.VMEM((8, KP, KP), BF16),
            pltpu.VMEM((8, KP, KP), BF16),
            pltpu.VMEM((3, rows, SPAN), F32),
            pltpu.VMEM((3, rows, SPAN), F32),
            pltpu.VMEM((SX * SD, SPAN), F32),
            pltpu.VMEM((SX * SD, SPAN), F32),
            pltpu.VMEM((SX * SD, SPAN), F32),
            pltpu.VMEM((SLOTS, TILES), BF16),
            pltpu.VMEM((SLOTS, SLOTS), BF16),
            pltpu.VMEM((8 * LEAVES, SLOTS), BF16),
            pltpu.VMEM((3, TILES, SPAN), F32),
            pltpu.VMEM((SPAN, SPAN), BF16),
            pltpu.VMEM((SWEEPS, 2, 3, SD, SPAN), BF16),
            pltpu.VMEM((SWEEPS, 2, 3, SD, SPAN), BF16),
            pltpu.VMEM((SWEEPS, 2, 3, SX, SPAN), BF16),
            pltpu.VMEM((SWEEPS, 2, 3, SX, SPAN), BF16),
            pltpu.VMEM((ND, 2 * NS, SPAN), BF16),
            pltpu.VMEM((ND, 2 * NS, SPAN), BF16),
            pltpu.VMEM((NS, 2 * ND, SPAN), BF16),
            pltpu.VMEM((NS, 2 * ND, SPAN), BF16),
            pltpu.VMEM((ND, 2 * NS, SPAN), BF16),
            pltpu.VMEM((ND, 2 * NS, SPAN), BF16),
            pltpu.VMEM((NS, 2 * ND, SPAN), BF16),
            pltpu.VMEM((NS, 2 * ND, SPAN), BF16),
            pltpu.VMEM((1, 3 * KP), F32),
            pltpu.VMEM((ND, 1, 3 * KP), F32),
            pltpu.VMEM((1, 5 * KP), F32),
            pltpu.VMEM((NS, 1, 5 * KP), F32),
            dma((8,)),
            dma((SWEEPS, 4)),
            dma((SWEEPS, 4)),
            dma((ND,)), dma((ND,)), dma((NS,)), dma((NS,)),
            dma((ND,)), dma((ND,)), dma((NS,)), dma((NS,)),
            dma((ND,)), dma((ND,)), dma((NS,)), dma((NS,)),
        ],
        compiler_params=pltpu.CompilerParams(
            collective_id=0, has_side_effects=True, vmem_limit_bytes=60 * 1024 * 1024
        ),
        cost_estimate=pl.CostEstimate(flops=10**8, bytes_accessed=12 * 10**6, transcendentals=0),
    )(
        tile_cell.reshape(1, TILES),
        leaf_octant.reshape(8, 8),
        node_octant.reshape(1, 8),
        subtree_octant.reshape(2, 8),
        cluster_octant,
        root_octant.reshape(1, 8),
        tile_owner.reshape(1, TILES),
        tile_class.reshape(1, TILES),
        tile_leaf.reshape(1, TILES),
        velocity,
        diffusion,
        advection,
        normals.reshape(3, TILES, SPAN),
        jnp.transpose(source_expansion, (2, 0, 1)).reshape(8 * COEF, SPAN),
        jnp.transpose(translation, (1, 0, 2)).reshape(8 * COEF, COEF),
    )
    return flow.reshape(3, SX, SD, SPAN), leaves.reshape(1, 1, LEAVES, COEF), upper


def solution(mesh):
    in_specs = (
        P(None, "stream", "depth", None),
        P("stream", "depth", None),
        P("stream", "depth", None),
        P("stream", "depth", None, None, None),
        P("stream", "depth", None),
        P("stream", "depth", None),
        P("stream", "depth", None),
        P("stream", "depth", None, None),
        P(),
        P(),
        P("stream", "depth", None, None),
        P("stream", "depth", None),
        P("stream", None, None),
        P(),
        P(),
    )
    out_specs = (P(None, "stream", "depth", None), P("stream", "depth", None, None), P())
    return jax.shard_map(
        per_device, mesh=mesh, in_specs=in_specs, out_specs=out_specs, check_vma=False
    )
```

profile of v0, /device:TPU:1, one launch (start us, length us, event | category | flops | bytes accessed | tf_op | source)
XLA Modules:
  0.0 72.6 jit_solution(13361842498786716469)
XLA Ops:
  0.6 65.8 %shard_map.166 = (f32[3,3072,128]{2,1,0:T(8,128)}, f32[64,289]{1,0:T(8,128)}, f32[19,289]{1,0:T(8,128)}) custom-call(s32[1,128]{1,0:T(1,128)} %bitcast.24, s32[8,8]{1,0:T(8,128)} %bitcast.22, s32[1,8]{1,0:T(1,128)} %bitcast.25, s32[2,8]{1,0:T(2,128)} %bitcast.23, s32[2,8]{1,0:T(2,128)} %coct.1, s32[1,8]{1,0:T(1,128)} %bitcast.26, s32[1,128]{1,0:T(1,128)} %bitcast.27, ...), custom_call_target="tpu_custom_call" | custom-call | flops 100000000 | bytes 12000000 | tf_op jit(solution)/shard_map/pallas_call | solution.py:416
  66.5 0.0 copy-start
  66.5 0.0 copy-start.1
  66.5 4.9 %copy.21 = f32[3,64,48,128]{3,2,1,0:T(8,128)} copy(f32[3,64,48,128]{3,2,1,0:T(8,128)} %bitcast.17) | data formatting | bytes 9437184
  71.3 0.0 copy-done
  71.4 0.6 copy.22
  72.0 0.0 copy-done.1
  72.0 0.6 copy.23
Async XLA Ops:
  66.5 4.9 %copy-start = (f32[64,289]{1,0:T(8,128)S(1)}, f32[64,289]{1,0:T(8,128)}, u32[]{:S(2)}) copy-start(f32[64,289]{1,0:T(8,128)} %get-tuple-element.7) | copy-start | bytes 221956
  66.5 5.5 %copy-start.1 = (f32[19,289]{1,0:T(8,128)S(1)}, f32[19,289]{1,0:T(8,128)}, u32[]{:S(2)}) copy-start(f32[19,289]{1,0:T(8,128)} %get-tuple-element.14) | copy-start | bytes 65896
where the time goes:
time: 72.8 us; the launch traced here: 72.6 us
  Pallas kernels  65.8 us (90%)
  local copies, waits for them, and re-layouts  6.12 us (8%)
    pallas_call x1, Pallas kernels, per_device(): pl.pallas_call(kernel, out_shape=(jax.ShapeDtypeStruct((3, SX * SD, SPAN)...  65.8 us
    unnamed x7, local copies, waits for them, and re-layouts  6.12 us

commit v1 on v0

--- a/solution.py
+++ b/solution.py
@@ -15,6 +15,7 @@
 KP = 384
 KR = 304
 SLOTS = 2 * NS * ND
+UNROLL = 16
 
 
 def split(value):
@@ -40,7 +41,7 @@
     vel, dif, adv, nrm, exp, tr,
     flow, leaves, upper,
     velv, difv, advv, nrmv, expv, trv, tv, ef, et, wh, wl, qa, qb, al, ka, be,
-    pmat, perm, gg, picked, order,
+    pmat, perm, gg, picked, order, beside,
     xs, xr, ds, dr, m1s, m1r, m2s, m2r, a1s, a1r, a2s, a2r, e1s, e1r, e2s, e2r,
     lsem, hss, hrs, m1ss, m1rs, m2ss, m2rs, a1ss, a1rs, a2ss, a2rs, e1ss, e1rs, e2ss, e2rs,
 ):
@@ -161,6 +162,8 @@
     feature = iota((SPAN, TILES), 0)
     meta = jnp.where((feature == leaf[...]) | (feature == cls[...] + LEAVES), 1.0, 0.0).astype(BF16)
     m1s[...] = dot_nt(pmat[...], meta).astype(BF16).reshape(ND, 2 * NS, SPAN)
+    apart = (iota((SPAN, SPAN), 0) - iota((SPAN, SPAN), 1)) & (SPAN - 1)
+    beside[...] = jnp.where((apart == 1) | (apart == SPAN - 1), 1.0, 0.0).astype(BF16)
     out = iota((SLOTS, SLOTS), 0)
     source = ((out >> 1) & (ND - 1)) * (2 * NS) + (out >> 5) * 2 + (out & 1)
     perm[...] = jnp.where(iota((SLOTS, SLOTS), 1) == source, 1.0, 0.0).astype(BF16)
@@ -194,22 +197,22 @@
     m1r[j] = m1s[j]
 
     def sweep(src, dst, pitch, lead):
+        slabs = src.reshape(3, SX + 2, SLAB, SPAN)
+
         def step(x, carry):
             rows = pl.ds(pl.multiple_of(x * SD, 8), SD)
             kappa, beta, alpha = ka[rows, :], be[rows, :], al[rows, :]
-            at = (x + 1) * SLAB + LEAD
             for k in range(3):
-                view = src.at[k]
-                c = view[pl.ds(pl.multiple_of(at, 8), SD), :]
-                f = view[pl.ds(pl.multiple_of(at + SLAB, 8), SD), :]
-                b = view[pl.ds(pl.multiple_of(at - SLAB, 8), SD), :]
-                up = view[pl.ds(at + 1, SD), :]
-                down = view[pl.ds(at - 1, SD), :]
-                total = f + (up + down) + (pltpu.roll(c, 1, 1) + pltpu.roll(c, SPAN - 1, 1))
+                c = slabs[k, x + 1, pl.ds(LEAD, SD), :]
+                f = slabs[k, x + 2, pl.ds(LEAD, SD), :]
+                b = slabs[k, x, pl.ds(LEAD, SD), :]
+                up = slabs[k, x + 1, pl.ds(LEAD + 1, SD), :]
+                down = slabs[k, x + 1, pl.ds(LEAD - 1, SD), :]
+                total = f + (up + down) + dot(c.astype(BF16), beside[...])
                 dst[k, pl.ds(pl.multiple_of(x * pitch + lead, 8), SD), :] = alpha * c + kappa * total + beta * b
             return carry
 
-        lax.fori_loop(0, SX, step, 0)
+        lax.fori_loop(0, SX, step, 0, unroll=UNROLL)
 
     def faces(n, dst, pitch, lead):
         first = pl.ds(lead, SD)
@@ -404,22 +407,27 @@
         sent(copies)
 
 
+def write_out(*refs):
+    copies = [pltpu.make_async_copy(refs[n], refs[n + 3], refs[6].at[n]) for n in range(3)]
+    for copy in copies:
+        copy.start()
+    for copy in copies:
+        copy.wait()
+
+
 def per_device(
     velocity, diffusion, advection, normals, tile_cell, tile_class, tile_leaf, tile_owner,
     source_expansion, translation, leaf_octant, node_octant, subtree_octant, cluster_octant, root_octant,
 ):
     smem = pl.BlockSpec(memory_space=pltpu.SMEM)
     vmem = pl.BlockSpec(memory_space=pltpu.VMEM)
-    hbm = pl.BlockSpec(memory_space=pl.ANY)
+    hbm = pl.BlockSpec(memory_space=pltpu.HBM)
     dma = pltpu.SemaphoreType.DMA
     rows = (SX + 2) * SLAB
-    flow, leaves, upper = pl.pallas_call(
+    shapes = ((3, SX * SD, SPAN), (LEAVES, COEF), (2 * NS + 3, COEF))
+    results = pl.pallas_call(
         kernel,
-        out_shape=(
-            jax.ShapeDtypeStruct((3, SX * SD, SPAN), F32),
-            jax.ShapeDtypeStruct((LEAVES, COEF), F32),
-            jax.ShapeDtypeStruct((2 * NS + 3, COEF), F32),
-        ),
+        out_shape=tuple(pltpu.VMEM(shape, F32) for shape in shapes),
         in_specs=[smem] * 6 + [vmem] * 3 + [hbm] * 6,
         out_specs=(vmem, vmem, vmem),
         scratch_shapes=[
@@ -443,6 +451,7 @@
             pltpu.VMEM((SLOTS, SLOTS), BF16),
             pltpu.VMEM((8 * LEAVES, SLOTS), BF16),
             pltpu.VMEM((3, TILES, SPAN), F32),
+            pltpu.VMEM((SPAN, SPAN), BF16),
             pltpu.VMEM((SPAN, SPAN), BF16),
             pltpu.VMEM((SWEEPS, 2, 3, SD, SPAN), BF16),
             pltpu.VMEM((SWEEPS, 2, 3, SD, SPAN), BF16),
@@ -468,7 +477,7 @@
             dma((ND,)), dma((ND,)), dma((NS,)), dma((NS,)),
         ],
         compiler_params=pltpu.CompilerParams(
-            collective_id=0, has_side_effects=True, vmem_limit_bytes=60 * 1024 * 1024
+            collective_id=0, has_side_effects=True, vmem_limit_bytes=60400 * 1024
         ),
         cost_estimate=pl.CostEstimate(flops=10**8, bytes_accessed=12 * 10**6, transcendentals=0),
     )(
@@ -488,6 +497,14 @@
         jnp.transpose(source_expansion, (2, 0, 1)).reshape(8 * COEF, SPAN),
         jnp.transpose(translation, (1, 0, 2)).reshape(8 * COEF, COEF),
     )
+    flow, leaves, upper = pl.pallas_call(
+        write_out,
+        out_shape=tuple(jax.ShapeDtypeStruct(shape, F32) for shape in shapes),
+        in_specs=[vmem] * 3,
+        out_specs=[hbm] * 3,
+        scratch_shapes=[dma((3,))],
+        compiler_params=pltpu.CompilerParams(vmem_limit_bytes=1024 * 1024),
+    )(*results)
     return flow.reshape(3, SX, SD, SPAN), leaves.reshape(1, 1, LEAVES, COEF), upper
 
 

time: 72.8 us -> 52.4 us (0.72)
  Pallas kernels: 65.8 us -> 51.6 us
  local copies, waits for them, and re-layouts: 6.12 us -> 0 us
    pallas_call x1 -> x2, Pallas kernels: 65.8 us -> 51.6 us  [the longest x1 49.4 us: per_device(): pl.pallas_call(kernel, out_shape=tuple((pltpu.VMEM(shape, F32) for shape...]
    unnamed x7 -> x0, local copies, waits for them, and re-layouts: 6.12 us -> none
where the time goes in v1:
time: 52.4 us; the launch traced here: 52.3 us
  Pallas kernels  51.6 us (98%)
  between operations  0.64 us (1%)
    pallas_call x1, Pallas kernels, per_device(): pl.pallas_call(kernel, out_shape=tuple((pltpu.VMEM(shape, F32) for shape...  49.4 us
    pallas_call x1, Pallas kernels, per_device(): pl.pallas_call(write_out, out_shape=tuple((jax.ShapeDtypeStruct(shape, F3...  2.23 us

profile of v1, /device:TPU:1, one launch (start us, length us, event | category | flops | bytes accessed | tf_op | source)
XLA Modules:
  0.0 52.3 jit_solution(5878204419530991824)
XLA Ops:
  0.6 49.4 %shard_map.166 = (f32[3,3072,128]{2,1,0:T(8,128)S(1)}, f32[64,289]{1,0:T(8,128)S(1)}, f32[19,289]{1,0:T(8,128)S(1)}) custom-call(s32[1,128]{1,0:T(1,128)} %bitcast.22, s32[8,8]{1,0:T(8,128)} %bitcast.20, s32[1,8]{1,0:T(1,128)} %bitcast.23, s32[2,8]{1,0:T(2,128)} %bitcast.21, s32[2,8]{1,0:T(2,128)} %coct.1, s32[1,8]{1,0:T(1,128)} %bitcast.24, ...), custom_call_target="tpu_custom_call" | custom-call | flops 100000000 | bytes 12000000 | tf_op jit(solution)/shard_map/pallas_call | solution.py:428
  50.1 2.2 %shard_map.167 = (f32[3,3072,128]{2,1,0:T(8,128)}, f32[64,289]{1,0:T(8,128)}, f32[19,289]{1,0:T(8,128)}) custom-call(f32[3,3072,128]{2,1,0:T(8,128)S(1)} %get-tuple-element.9.refs_0_, f32[64,289]{1,0:T(8,128)S(1)} %get-tuple-element.10.refs_1_, f32[19,289]{1,0:T(8,128)S(1)} %get-tuple-element.11.refs_2_), custom_call_target="tpu_custom_call" | custom-call | tf_op jit(solution)/shard_map/pallas_call | solution.py:500

commit v2 on v1

--- a/solution.py
+++ b/solution.py
@@ -16,6 +16,7 @@
 KR = 304
 SLOTS = 2 * NS * ND
 UNROLL = 16
+PARTS = 2
 
 
 def split(value):
@@ -31,62 +32,77 @@
     return lax.dot_general(a, b, (((1,), (1,)), ((), ())), preferred_element_type=F32)
 
 
+DEPTH_ORDER = (10, 9, 11, 6, 14, 5, 7, 13, 15, 8, 2, 4, 12, 1, 3)
+STREAM_ORDER = (5, 4, 3, 7, 2, 6, 1)
+
+
+def flip(value, bits):
+    if bits == 0:
+        return value
+    if bits == 1:
+        return value + 1 - 2 * lax.rem(value, 2)
+    if bits == 2:
+        return lax.rem(value + 2, 4)
+    return 3 - value
+
+
 def iota(shape, dim):
     return lax.broadcasted_iota(I32, shape, dim)
 
 
 def kernel(
-    cell, loct, noct, soct, coct, roct,
-    owner, cls, leaf,
+    cell_in, loct_in, noct_in, soct_in, coct_in, roct_in, owner_in, cls_in, leaf_in,
     vel, dif, adv, nrm, exp, tr,
     flow, leaves, upper,
+    cell, loct, noct, soct, coct, roct, owner, cls, leaf,
     velv, difv, advv, nrmv, expv, trv, tv, ef, et, wh, wl, qa, qb, al, ka, be,
-    pmat, perm, gg, picked, order, beside,
+    pmat, perm, gg, picked, order, beside, lifth, liftl,
     xs, xr, ds, dr, m1s, m1r, m2s, m2r, a1s, a1r, a2s, a2r, e1s, e1r, e2s, e2r,
-    lsem, hss, hrs, m1ss, m1rs, m2ss, m2rs, a1ss, a1rs, a2ss, a2rs, e1ss, e1rs, e2ss, e2rs,
+    fsem, lsem, hss, hrs, m1ss, m1rs, m2ss, m2rs, a1ss, a1rs, a2ss, a2rs, e1ss, e1rs, e2ss, e2rs,
 ):
     i, j = lax.axis_index("stream"), lax.axis_index("depth")
 
-    loads = [
-        pltpu.make_async_copy(s, d, lsem.at[n])
-        for n, (s, d) in enumerate(
-            (
-                (vel, velv),
-                (dif, difv),
-                (adv, advv),
-                (nrm, nrmv),
-                (exp, expv),
-                (tr.at[:, pl.ds(0, SPAN)], tv.at[0, pl.ds(0, 8 * COEF), :]),
-                (tr.at[:, pl.ds(SPAN, SPAN)], tv.at[1, pl.ds(0, 8 * COEF), :]),
-                (tr.at[:, pl.ds(2 * SPAN, COEF - 2 * SPAN)], trv),
-            )
-        )
+    def in_depth(r):
+        return 4 * flip(lax.div(j, 4), r // 4) + flip(lax.rem(j, 4), r % 4)
+
+    def in_stream(r):
+        core = lax.rem(i, 2)
+        return 2 * flip(lax.div(i, 2), r // 2) + (1 - core if r % 2 else core)
+
+    barrier = pltpu.get_barrier_semaphore()
+    for r in DEPTH_ORDER:
+        pl.semaphore_signal(barrier, inc=1, device_id=(i, in_depth(r)), device_id_type=MESH)
+    for r in STREAM_ORDER:
+        pl.semaphore_signal(barrier, inc=1, device_id=(in_stream(r), j), device_id_type=MESH)
+
+    def part(src, dst, n, p):
+        rows = pl.ds(p * (SX // PARTS), SX // PARTS)
+        at = (slice(None), rows) if len(src.shape) == 4 else (rows,)
+        return pltpu.make_async_copy(src.at[at], dst.at[at], fsem.at[n, p])
+
+    field_loads = [
+        [part(s, d, n, p) for n, (s, d) in enumerate(((vel, velv), (dif, difv), (adv, advv)))] for p in range(PARTS)
     ]
-    for copy in loads:
-        copy.start()
-
-    barrier = pltpu.get_barrier_semaphore()
-    for r in range(1, ND):
-        pl.semaphore_signal(barrier, inc=1, device_id=(i, lax.rem(j + r, ND)), device_id_type=MESH)
-    for r in range(1, NS):
-        pl.semaphore_signal(barrier, inc=1, device_id=(lax.rem(i + r, NS), j), device_id_type=MESH)
+    for copies in field_loads:
+        for copy in copies:
+            copy.start()
 
     def along_depth(src, dst, ss, rs):
         return [
             pltpu.make_async_remote_copy(
-                src_ref=src(lax.rem(j + r, ND)), dst_ref=dst.at[j], send_sem=ss.at[r], recv_sem=rs.at[r],
-                device_id=(i, lax.rem(j + r, ND)), device_id_type=MESH,
+                src_ref=src(in_depth(r)), dst_ref=dst.at[j], send_sem=ss.at[r], recv_sem=rs.at[r],
+                device_id=(i, in_depth(r)), device_id_type=MESH,
             )
-            for r in range(1, ND)
+            for r in DEPTH_ORDER
         ]
 
     def along_stream(src, dst, ss, rs):
         return [
             pltpu.make_async_remote_copy(
-                src_ref=src(lax.rem(i + r, NS)), dst_ref=dst.at[i], send_sem=ss.at[r], recv_sem=rs.at[r],
-                device_id=(lax.rem(i + r, NS), j), device_id_type=MESH,
+                src_ref=src(in_stream(r)), dst_ref=dst.at[i], send_sem=ss.at[r], recv_sem=rs.at[r],
+                device_id=(in_stream(r), j), device_id_type=MESH,
             )
-            for r in range(1, NS)
+            for r in STREAM_ORDER
         ]
 
     def start(copies):
@@ -101,34 +117,35 @@
         for copy in copies:
             copy.wait_send()
 
-    def halo(n):
-        xlow = velv.at[:, 0] if n == 0 else xs.at[n, 0]
-        xhigh = velv.at[:, SX - 1] if n == 0 else xs.at[n, 1]
+    def halo(n, k):
+        xlow = velv.at[k, 0] if n == 0 else xs.at[n, 0, k]
+        xhigh = velv.at[k, SX - 1] if n == 0 else xs.at[n, 1, k]
 
         def copy(src, dst, which, device):
             return pltpu.make_async_remote_copy(
-                src_ref=src, dst_ref=dst, send_sem=hss.at[n, which], recv_sem=hrs.at[n, which],
+                src_ref=src, dst_ref=dst, send_sem=hss.at[n, which, k], recv_sem=hrs.at[n, which, k],
                 device_id=device, device_id_type=MESH,
             )
 
         return (
-            (i < NS - 1, i > 0, copy(xhigh, xr.at[n, 0], 0, (lax.rem(i + 1, NS), j))),
-            (i > 0, i < NS - 1, copy(xlow, xr.at[n, 1], 1, (lax.rem(i + NS - 1, NS), j))),
-            (j < ND - 1, j > 0, copy(ds.at[n, 1], dr.at[n, 0], 2, (i, lax.rem(j + 1, ND)))),
-            (j > 0, j < ND - 1, copy(ds.at[n, 0], dr.at[n, 1], 3, (i, lax.rem(j + ND - 1, ND)))),
+            (j < ND - 1, j > 0, copy(ds.at[n, 1, k], dr.at[n, 0, k], 2, (i, lax.rem(j + 1, ND)))),
+            (j > 0, j < ND - 1, copy(ds.at[n, 0, k], dr.at[n, 1, k], 3, (i, lax.rem(j + ND - 1, ND)))),
+            (i < NS - 1, i > 0, copy(xhigh, xr.at[n, 0, k], 0, (lax.rem(i + 1, NS), j))),
+            (i > 0, i < NS - 1, copy(xlow, xr.at[n, 1, k], 1, (lax.rem(i + NS - 1, NS), j))),
         )
 
-    def halo_start(n):
-        for send, _, copy in halo(n):
+    def halo_start(n, k):
+        for send, _, copy in halo(n, k):
             pl.when(send)(copy.start)
 
-    def halo_arrive(n):
-        for _, receive, copy in halo(n):
+    def halo_arrive(n, k):
+        for _, receive, copy in halo(n, k):
             pl.when(receive)(copy.wait_recv)
 
     def halo_sent(n):
-        for send, _, copy in halo(n):
-            pl.when(send)(copy.wait_send)
+        for k in range(3):
+            for send, _, copy in halo(n, k):
+                pl.when(send)(copy.wait_send)
 
     for edge, ref, side in ((i == 0, xr, 0), (i == NS - 1, xr, 1), (j == 0, dr, 0), (j == ND - 1, dr, 1)):
 
@@ -152,24 +169,9 @@
 
     lax.fori_loop(1, SX + 1, clear, 0)
 
-    own = owner[...]
-    across = jnp.broadcast_to(own.astype(F32), (TILES, TILES))
-    down = jnp.transpose(across)
-    before = iota((TILES, TILES), 0) < iota((TILES, TILES), 1)
-    rank = jnp.sum(jnp.where((across == down) & before, 1.0, 0.0), axis=0, keepdims=True).astype(I32)
-    slot = (own & (ND - 1)) * (2 * NS) + (own >> 4) * 2 + rank
-    pmat[...] = jnp.where(iota((SLOTS, TILES), 0) == slot, 1.0, 0.0).astype(BF16)
-    feature = iota((SPAN, TILES), 0)
-    meta = jnp.where((feature == leaf[...]) | (feature == cls[...] + LEAVES), 1.0, 0.0).astype(BF16)
-    m1s[...] = dot_nt(pmat[...], meta).astype(BF16).reshape(ND, 2 * NS, SPAN)
     apart = (iota((SPAN, SPAN), 0) - iota((SPAN, SPAN), 1)) & (SPAN - 1)
     beside[...] = jnp.where((apart == 1) | (apart == SPAN - 1), 1.0, 0.0).astype(BF16)
-    out = iota((SLOTS, SLOTS), 0)
-    source = ((out >> 1) & (ND - 1)) * (2 * NS) + (out >> 5) * 2 + (out & 1)
-    perm[...] = jnp.where(iota((SLOTS, SLOTS), 1) == source, 1.0, 0.0).astype(BF16)
-
-    for copy in loads[:3]:
-        copy.wait()
+
 
     def widen(x, carry):
         at = pl.multiple_of((x + 1) * SLAB + LEAD, 8)
@@ -183,7 +185,31 @@
         al[rows, :] = 1.0 - 6.0 * kappa - speed
         return carry
 
-    lax.fori_loop(0, SX, widen, 0)
+    for p, copies in enumerate(field_loads):
+        for copy in copies:
+            copy.wait()
+        lax.fori_loop(p * (SX // PARTS), (p + 1) * (SX // PARTS), widen, 0, unroll=4)
+    loads = [
+        pltpu.make_async_copy(s, d, lsem.at[n])
+        for n, (s, d) in enumerate(
+            (
+                (owner_in, owner),
+                (cls_in, cls),
+                (leaf_in, leaf),
+                (cell_in, cell),
+                (loct_in, loct),
+                (noct_in, noct),
+                (soct_in, soct),
+                (coct_in, coct),
+                (roct_in, roct),
+                (nrm, nrmv),
+                (exp, expv),
+                (tr.at[:, pl.ds(0, SPAN)], tv.at[0, pl.ds(0, 8 * COEF), :]),
+                (tr.at[:, pl.ds(SPAN, SPAN)], tv.at[1, pl.ds(0, 8 * COEF), :]),
+                (tr.at[:, pl.ds(2 * SPAN, COEF - 2 * SPAN)], trv),
+            )
+        )
+    ]
     low = pl.ds(SLAB + LEAD, SX, stride=SLAB)
     high = pl.ds(SLAB + LEAD + SD - 1, SX, stride=SLAB)
     for k in range(3):
@@ -191,7 +217,27 @@
         ds[0, 1, k] = qa[k, high, :].astype(BF16)
 
     pl.semaphore_wait(barrier, ND - 1 + NS - 1)
-    halo_start(0)
+    for k in range(3):
+        halo_start(0, k)
+    for copy in loads:
+        copy.start()
+
+    for copy in loads[:9]:
+        copy.wait()
+    own = owner[...]
+    across = jnp.broadcast_to(own.astype(F32), (TILES, TILES))
+    down = jnp.transpose(across)
+    before = iota((TILES, TILES), 0) < iota((TILES, TILES), 1)
+    rank = jnp.sum(jnp.where((across == down) & before, 1.0, 0.0), axis=0, keepdims=True).astype(I32)
+    slot = (own & (ND - 1)) * (2 * NS) + (own >> 4) * 2 + rank
+    pmat[...] = jnp.where(iota((SLOTS, TILES), 0) == slot, 1.0, 0.0).astype(BF16)
+    feature = iota((SPAN, TILES), 0)
+    meta = jnp.where((feature == leaf[...]) | (feature == cls[...] + LEAVES), 1.0, 0.0).astype(BF16)
+    m1s[...] = dot_nt(pmat[...], meta).astype(BF16).reshape(ND, 2 * NS, SPAN)
+    out = iota((SLOTS, SLOTS), 0)
+    source = ((out >> 1) & (ND - 1)) * (2 * NS) + (out >> 5) * 2 + (out & 1)
+    perm[...] = jnp.where(iota((SLOTS, SLOTS), 1) == source, 1.0, 0.0).astype(BF16)
+
     meta1 = along_depth(lambda p: m1s.at[p], m1r, m1ss, m1rs)
     start(meta1)
     m1r[j] = m1s[j]
@@ -222,8 +268,11 @@
         klow = ka[pl.ds(0, SX, stride=SD), :]
         khigh = ka[pl.ds(SD - 1, SX, stride=SD), :]
         for k in range(3):
-            dst[k, first, :] = dst[k, first, :] + be[pl.ds(0, SD), :] * xr[n, 0, k].astype(F32)
-            dst[k, last, :] = dst[k, last, :] + ka[pl.ds((SX - 1) * SD, SD), :] * xr[n, 1, k].astype(F32)
+            halo_arrive(n, k)
+            qf = dst[k, first, :] + be[pl.ds(0, SD), :] * xr[n, 0, k].astype(F32)
+            ql = dst[k, last, :] + ka[pl.ds((SX - 1) * SD, SD), :] * xr[n, 1, k].astype(F32)
+            dst[k, first, :] = qf
+            dst[k, last, :] = ql
             ql = dst[k, low, :] + klow * dr[n, 0, k].astype(F32)
             qh = dst[k, high, :] + khigh * dr[n, 1, k].astype(F32)
             dst[k, low, :] = ql
@@ -233,11 +282,54 @@
                 ds[n + 1, 1, k] = qh.astype(BF16)
                 xs[n + 1, 0, k] = dst[k, first, :].astype(BF16)
                 xs[n + 1, 1, k] = dst[k, last, :].astype(BF16)
-        if n + 1 < SWEEPS:
-            halo_start(n + 1)
+                halo_start(n + 1, k)
 
     sweep(qa, qb, SLAB, SLAB + LEAD)
-    for copy in loads[5:]:
+    faces(0, qb, SLAB, SLAB + LEAD)
+
+    sweep(qb, qa, SLAB, SLAB + LEAD)
+    arrive(meta1)
+    m2s[...] = dot(perm[...], m1r[...].reshape(SLOTS, SPAN)).astype(BF16).reshape(NS, 2 * ND, SPAN)
+    meta2 = along_stream(lambda p: m2s.at[p], m2r, m2ss, m2rs)
+    start(meta2)
+    m2r[i] = m2s[i]
+    faces(1, qa, SLAB, SLAB + LEAD)
+
+    sweep(qa, qb, SLAB, SLAB + LEAD)
+    faces(2, qb, SLAB, SLAB + LEAD)
+
+    sweep(qb, flow, SD, 0)
+    faces(3, flow, SD, 0)
+
+    loads[9].wait()
+
+    def sample(t, carry):
+        for k in range(3):
+            picked[k, t] = flow[k, cell[0, t]]
+        return carry
+
+    lax.fori_loop(0, TILES, sample, 0, unroll=8)
+    strength = nrmv[0].astype(F32) * picked[0]
+    for k in (1, 2):
+        strength = strength + nrmv[k].astype(F32) * picked[k]
+    a1s[...] = dot(pmat[...], strength.astype(BF16)).astype(BF16).reshape(ND, 2 * NS, SPAN)
+    data1 = along_depth(lambda p: a1s.at[p], a1r, a1ss, a1rs)
+    start(data1)
+    a1r[j] = a1s[j]
+
+    loads[10].wait()
+    et[pl.ds(KR, KP - KR), :] = jnp.zeros((KP - KR, 8 * SPAN), BF16)
+    ef[pl.ds(0, 8 * COEF), :] = expv[...].astype(F32)
+    ef[pl.ds(8 * COEF, 8 * (KR - COEF)), :] = jnp.zeros((8 * (KR - COEF), SPAN), F32)
+
+    def classes(b, carry):
+        for c in range(8):
+            value = ef[pl.ds(b * 128 + c, 16, stride=8), :]
+            et[pl.ds(pl.multiple_of(b * 16, 16), 16), pl.ds(c * SPAN, SPAN)] = value.astype(BF16)
+        return carry
+
+    lax.fori_loop(0, KR // 16, classes, 0)
+    for copy in loads[11:]:
         copy.wait()
     for w in (wh, wl):
         for o in range(8):
@@ -259,31 +351,6 @@
         return carry
 
     lax.fori_loop(0, KR // 16, halve, 0)
-    halo_arrive(0)
-    faces(0, qb, SLAB, SLAB + LEAD)
-
-    sweep(qb, qa, SLAB, SLAB + LEAD)
-    arrive(meta1)
-    m2s[...] = dot(perm[...], m1r[...].reshape(SLOTS, SPAN)).astype(BF16).reshape(NS, 2 * ND, SPAN)
-    meta2 = along_stream(lambda p: m2s.at[p], m2r, m2ss, m2rs)
-    start(meta2)
-    m2r[i] = m2s[i]
-    loads[4].wait()
-    et[pl.ds(KR, KP - KR), :] = jnp.zeros((KP - KR, 8 * SPAN), BF16)
-    ef[pl.ds(0, 8 * COEF), :] = expv[...].astype(F32)
-    ef[pl.ds(8 * COEF, 8 * (KR - COEF)), :] = jnp.zeros((8 * (KR - COEF), SPAN), F32)
-
-    def classes(b, carry):
-        for c in range(8):
-            value = ef[pl.ds(b * 128 + c, 16, stride=8), :]
-            et[pl.ds(pl.multiple_of(b * 16, 16), 16), pl.ds(c * SPAN, SPAN)] = value.astype(BF16)
-        return carry
-
-    lax.fori_loop(0, KR // 16, classes, 0)
-    halo_arrive(1)
-    faces(1, qa, SLAB, SLAB + LEAD)
-
-    sweep(qa, qb, SLAB, SLAB + LEAD)
     arrive(meta2)
     lane = iota((1, SPAN), 1)
     octant = jnp.full((1, SPAN), -1, I32)
@@ -298,33 +365,23 @@
     class_of = dot_nt(pick, arrived)
     for c in range(8):
         gg[pl.ds(c * LEAVES, LEAVES), :] = (leaf_of * class_of[c : c + 1, :]).astype(BF16)
-    halo_arrive(2)
-    faces(2, qb, SLAB, SLAB + LEAD)
-
-    sweep(qb, flow, SD, 0)
-    halo_arrive(3)
-    faces(3, flow, SD, 0)
-
-    loads[3].wait()
-
-    def sample(t, carry):
-        for k in range(3):
-            picked[k, t] = flow[k, cell[0, t]]
-        return carry
-
-    lax.fori_loop(0, TILES, sample, 0, unroll=8)
-    strength = nrmv[0].astype(F32) * picked[0]
-    for k in (1, 2):
-        strength = strength + nrmv[k].astype(F32) * picked[k]
-    a1s[...] = dot(pmat[...], strength.astype(BF16)).astype(BF16).reshape(ND, 2 * NS, SPAN)
-    data1 = along_depth(lambda p: a1s.at[p], a1r, a1ss, a1rs)
-    start(data1)
-    a1r[j] = a1s[j]
     arrive(data1)
     a2s[...] = dot(perm[...], a1r[...].reshape(SLOTS, SPAN)).astype(BF16).reshape(NS, 2 * ND, SPAN)
     data2 = along_stream(lambda p: a2s.at[p], a2r, a2ss, a2rs)
     start(data2)
     a2r[i] = a2s[i]
+
+    group, member = lax.div(j, 8), lax.rem(j, 8)
+    table = soct[group, member]
+    high, low = wh[table], wl[table]
+    lifth[:, :KP] = high
+    liftl[:, :KP] = low
+    for n, table in ((1, coct[group, i]), (2, roct[0, group])):
+        following = wh[table]
+        h, l = split(dot(high, following) + dot(low, following) + dot(high, wl[table]))
+        high, low = h.astype(BF16), l.astype(BF16)
+        lifth[:, pl.ds(n * KP, KP)] = high
+        liftl[:, pl.ds(n * KP, KP)] = low
     arrive(data2)
 
     sums = dot(gg[...], a2r[...].reshape(SLOTS, SPAN))
@@ -349,18 +406,10 @@
     lhs = jnp.concatenate([jnp.where(octant == o, stacked, 0.0).astype(BF16) for o in range(8)], axis=1)
     subtree = jnp.sum(dot(lhs, wh[...].reshape(8 * KP, KP)) + dot(lhs, wl[...].reshape(8 * KP, KP)), axis=0, keepdims=True)
 
-    group, member = j >> 3, j & 7
-
-    def lift(vector, which):
-        h, l = split(vector)
-        place = iota((16, KP), 0)
-        rows = jnp.where(place == 0, h, jnp.where(place == 1, l, 0.0)).astype(BF16)
-        return jnp.sum(dot(rows, wh[which]) + dot(rows, wl[which]), axis=0, keepdims=True)
-
-    in_cluster = lift(subtree, soct[group, member])
-    in_half = lift(in_cluster, coct[group, i])
-    in_root = lift(in_half, roct[0, group])
-    e1s[...] = jnp.concatenate([in_cluster, in_half, in_root], axis=1)
+    h, l = split(subtree)
+    place = iota((16, KP), 0)
+    lhs = jnp.where(place == 0, h, jnp.where(place == 1, l, 0.0)).astype(BF16)
+    e1s[...] = jnp.sum(dot(lhs, lifth[...]) + dot(lhs, liftl[...]), axis=0, keepdims=True)
     terms = along_depth(lambda p: e1s, e1r, e1ss, e1rs)
     start(terms)
     e1r[j] = e1s[...]
@@ -419,7 +468,6 @@
     velocity, diffusion, advection, normals, tile_cell, tile_class, tile_leaf, tile_owner,
     source_expansion, translation, leaf_octant, node_octant, subtree_octant, cluster_octant, root_octant,
 ):
-    smem = pl.BlockSpec(memory_space=pltpu.SMEM)
     vmem = pl.BlockSpec(memory_space=pltpu.VMEM)
     hbm = pl.BlockSpec(memory_space=pltpu.HBM)
     dma = pltpu.SemaphoreType.DMA
@@ -428,9 +476,18 @@
     results = pl.pallas_call(
         kernel,
         out_shape=tuple(pltpu.VMEM(shape, F32) for shape in shapes),
-        in_specs=[smem] * 6 + [vmem] * 3 + [hbm] * 6,
+        in_specs=[hbm] * 15,
         out_specs=(vmem, vmem, vmem),
         scratch_shapes=[
+            pltpu.SMEM((1, TILES), I32),
+            pltpu.SMEM((8, 8), I32),
+            pltpu.SMEM((1, 8), I32),
+            pltpu.SMEM((2, 8), I32),
+            pltpu.SMEM((2, 8), I32),
+            pltpu.SMEM((1, 8), I32),
+            pltpu.VMEM((1, TILES), I32),
+            pltpu.VMEM((1, TILES), I32),
+            pltpu.VMEM((1, TILES), I32),
             pltpu.VMEM((3, SX, SD, SPAN), BF16),
             pltpu.VMEM((SX, SD, SPAN), BF16),
             pltpu.VMEM((SX, SD, SPAN), BF16),
@@ -453,6 +510,8 @@
             pltpu.VMEM((3, TILES, SPAN), F32),
             pltpu.VMEM((SPAN, SPAN), BF16),
             pltpu.VMEM((SPAN, SPAN), BF16),
+            pltpu.VMEM((KP, 3 * KP), BF16),
+            pltpu.VMEM((KP, 3 * KP), BF16),
             pltpu.VMEM((SWEEPS, 2, 3, SD, SPAN), BF16),
             pltpu.VMEM((SWEEPS, 2, 3, SD, SPAN), BF16),
             pltpu.VMEM((SWEEPS, 2, 3, SX, SPAN), BF16),
@@ -469,9 +528,10 @@
             pltpu.VMEM((ND, 1, 3 * KP), F32),
             pltpu.VMEM((1, 5 * KP), F32),
             pltpu.VMEM((NS, 1, 5 * KP), F32),
-            dma((8,)),
-            dma((SWEEPS, 4)),
-            dma((SWEEPS, 4)),
+            dma((3, PARTS)),
+            dma((14,)),
+            dma((SWEEPS, 4, 3)),
+            dma((SWEEPS, 4, 3)),
             dma((ND,)), dma((ND,)), dma((NS,)), dma((NS,)),
             dma((ND,)), dma((ND,)), dma((NS,)), dma((NS,)),
             dma((ND,)), dma((ND,)), dma((NS,)), dma((NS,)),

time: 52.4 us -> 49.9 us (0.952)
  Pallas kernels: 51.6 us -> 49.1 us
    pallas_call x1, Pallas kernels: 49.4 us -> 46.9 us  [per_device(): pl.pallas_call(kernel, out_shape=tuple((pltpu.VMEM(shape, F32) for shape...]
where the time goes in v2:
time: 49.9 us; the launch traced here: 49.8 us
  Pallas kernels  49.1 us (98%)
  between operations  0.64 us (1%)
    pallas_call x1, Pallas kernels, per_device(): pl.pallas_call(kernel, out_shape=tuple((pltpu.VMEM(shape, F32) for shape...  46.9 us
    pallas_call x1, Pallas kernels, per_device(): pl.pallas_call(write_out, out_shape=tuple((jax.ShapeDtypeStruct(shape, F3...  2.23 us

profile of v2, /device:TPU:1, one launch (start us, length us, event | category | flops | bytes accessed | tf_op | source)
XLA Modules:
  0.0 49.8 jit_solution(18004950699706328513)
XLA Ops:
  0.6 46.9 %shard_map.166 = (f32[3,3072,128]{2,1,0:T(8,128)S(1)}, f32[64,289]{1,0:T(8,128)S(1)}, f32[19,289]{1,0:T(8,128)S(1)}) custom-call(s32[1,128]{1,0:T(1,128)} %bitcast.22, s32[8,8]{1,0:T(8,128)} %bitcast.20, s32[1,8]{1,0:T(1,128)} %bitcast.23, s32[2,8]{1,0:T(2,128)} %bitcast.21, s32[2,8]{1,0:T(2,128)} %coct_in.1, s32[1,8]{1,0:T(1,128)} %bitcast.24, ...), custom_call_target="tpu_custom_call" | custom-call | flops 100000000 | bytes 12000000 | tf_op jit(solution)/shard_map/pallas_call | solution.py:476
  47.5 2.2 %shard_map.167 = (f32[3,3072,128]{2,1,0:T(8,128)}, f32[64,289]{1,0:T(8,128)}, f32[19,289]{1,0:T(8,128)}) custom-call(f32[3,3072,128]{2,1,0:T(8,128)S(1)} %get-tuple-element.9.refs_0_, f32[64,289]{1,0:T(8,128)S(1)} %get-tuple-element.10.refs_1_, f32[19,289]{1,0:T(8,128)S(1)} %get-tuple-element.11.refs_2_), custom_call_target="tpu_custom_call" | custom-call | tf_op jit(solution)/shard_map/pallas_call | solution.py:560

commit v3 on v2

--- a/solution.py
+++ b/solution.py
@@ -55,8 +55,8 @@
     vel, dif, adv, nrm, exp, tr,
     flow, leaves, upper,
     cell, loct, noct, soct, coct, roct, owner, cls, leaf,
-    velv, difv, advv, nrmv, expv, trv, tv, ef, et, wh, wl, qa, qb, al, ka, be,
-    pmat, perm, gg, picked, order, beside, lifth, liftl,
+    velv, difv, advv, nrmv, expv, trv, tv, ef, et, w, qa, qb, al, ka, be,
+    pmat, perm, gg, picked, order, beside, lifts,
     xs, xr, ds, dr, m1s, m1r, m2s, m2r, a1s, a1r, a2s, a2r, e1s, e1r, e2s, e2r,
     fsem, lsem, hss, hrs, m1ss, m1rs, m2ss, m2rs, a1ss, a1rs, a2ss, a2rs, e1ss, e1rs, e2ss, e2rs,
 ):
@@ -318,22 +318,20 @@
     a1r[j] = a1s[j]
 
     loads[10].wait()
-    et[pl.ds(KR, KP - KR), :] = jnp.zeros((KP - KR, 8 * SPAN), BF16)
     ef[pl.ds(0, 8 * COEF), :] = expv[...].astype(F32)
-    ef[pl.ds(8 * COEF, 8 * (KR - COEF)), :] = jnp.zeros((8 * (KR - COEF), SPAN), F32)
-
-    def classes(b, carry):
-        for c in range(8):
-            value = ef[pl.ds(b * 128 + c, 16, stride=8), :]
-            et[pl.ds(pl.multiple_of(b * 16, 16), 16), pl.ds(c * SPAN, SPAN)] = value.astype(BF16)
+    ef[pl.ds(8 * COEF, 8 * (KP - COEF)), :] = jnp.zeros((8 * (KP - COEF), SPAN), F32)
+
+    def classes(c, carry):
+        for n in range(3):
+            value = jnp.transpose(ef[pl.ds(8 * SPAN * n + c, SPAN, stride=8), :])
+            et[pl.ds(pl.multiple_of(c * SPAN, SPAN), SPAN), pl.ds(n * SPAN, SPAN)] = value.astype(BF16)
         return carry
 
-    lax.fori_loop(0, KR // 16, classes, 0)
+    lax.fori_loop(0, 8, classes, 0)
     for copy in loads[11:]:
         copy.wait()
-    for w in (wh, wl):
-        for o in range(8):
-            w[o, pl.ds(KR, KP - KR), :] = jnp.zeros((KP - KR, KP), BF16)
+    for o in range(8):
+        w[o, pl.ds(KR, KP - KR), :] = jnp.zeros((KP - KR, 2 * KP), BF16)
     tv[:, pl.ds(8 * COEF, 8 * (KR - COEF)), :] = jnp.zeros((3, 8 * (KR - COEF), SPAN), F32)
     tv[2, pl.ds(0, 8 * COEF), :] = jnp.concatenate(
         [trv[...], jnp.zeros((8 * COEF, KP - COEF), F32)], axis=1
@@ -346,8 +344,8 @@
             for n in range(3):
                 lanes = pl.ds(n * SPAN, SPAN)
                 h, l = split(tv[n, rows, :])
-                wh[o, to, lanes] = h.astype(BF16)
-                wl[o, to, lanes] = l.astype(BF16)
+                w[o, to, lanes] = h.astype(BF16)
+                w[o, to, pl.ds(KP + n * SPAN, SPAN)] = l.astype(BF16)
         return carry
 
     lax.fori_loop(0, KR // 16, halve, 0)
@@ -373,15 +371,15 @@
 
     group, member = lax.div(j, 8), lax.rem(j, 8)
     table = soct[group, member]
-    high, low = wh[table], wl[table]
-    lifth[:, :KP] = high
-    liftl[:, :KP] = low
+    high, low = w[table][:, :KP], w[table][:, KP:]
+    lifts[:, :KP] = high
+    lifts[:, pl.ds(3 * KP, KP)] = low
     for n, table in ((1, coct[group, i]), (2, roct[0, group])):
-        following = wh[table]
-        h, l = split(dot(high, following) + dot(low, following) + dot(high, wl[table]))
+        following = w[table]
+        h, l = split(dot(high, following[:, :KP]) + dot(low, following[:, :KP]) + dot(high, following[:, KP:]))
         high, low = h.astype(BF16), l.astype(BF16)
-        lifth[:, pl.ds(n * KP, KP)] = high
-        liftl[:, pl.ds(n * KP, KP)] = low
+        lifts[:, pl.ds(n * KP, KP)] = high
+        lifts[:, pl.ds((3 + n) * KP, KP)] = low
     arrive(data2)
 
     sums = dot(gg[...], a2r[...].reshape(SLOTS, SPAN))
@@ -389,27 +387,30 @@
     for c in range(8):
         h, l = split(sums[c * LEAVES : (c + 1) * LEAVES])
         blocks.append(jnp.concatenate([h, l], axis=0).astype(BF16))
-    both = dot_nt(jnp.concatenate(blocks, axis=1), et[...])
+    both = dot(jnp.concatenate(blocks, axis=1), et[...])
     ordered_leaves = both[:LEAVES] + both[LEAVES:]
 
     h, l = split(ordered_leaves)
     lhs = jnp.concatenate(
         [jnp.concatenate([h[8 * o : 8 * o + 8], l[8 * o : 8 * o + 8]], axis=0).astype(BF16) for o in range(8)], axis=1
     )
-    product = dot(lhs, wh[...].reshape(8 * KP, KP)) + dot(lhs, wl[...].reshape(8 * KP, KP))
-    h, l = split(product[:8] + product[8:])
+    product = dot(lhs, w[...].reshape(8 * KP, 2 * KP))
+    product = product[:8] + product[8:]
+    h, l = split(product[:, :KP] + product[:, KP:])
     node = iota((16, KP), 0) & 7
     octant = jnp.full((16, KP), -1, I32)
     for p in range(8):
         octant = jnp.where(node == p, noct[0, p], octant)
     stacked = jnp.concatenate([h, l], axis=0)
     lhs = jnp.concatenate([jnp.where(octant == o, stacked, 0.0).astype(BF16) for o in range(8)], axis=1)
-    subtree = jnp.sum(dot(lhs, wh[...].reshape(8 * KP, KP)) + dot(lhs, wl[...].reshape(8 * KP, KP)), axis=0, keepdims=True)
+    product = dot(lhs, w[...].reshape(8 * KP, 2 * KP))
+    subtree = jnp.sum(product[:, :KP] + product[:, KP:], axis=0, keepdims=True)
 
     h, l = split(subtree)
     place = iota((16, KP), 0)
     lhs = jnp.where(place == 0, h, jnp.where(place == 1, l, 0.0)).astype(BF16)
-    e1s[...] = jnp.sum(dot(lhs, lifth[...]) + dot(lhs, liftl[...]), axis=0, keepdims=True)
+    product = dot(lhs, lifts[...])
+    e1s[...] = jnp.sum(product[:, : 3 * KP] + product[:, 3 * KP :], axis=0, keepdims=True)
     terms = along_depth(lambda p: e1s, e1r, e1ss, e1rs)
     start(terms)
     e1r[j] = e1s[...]
@@ -495,10 +496,9 @@
             pltpu.VMEM((8 * COEF, SPAN), BF16),
             pltpu.VMEM((8 * COEF, COEF - 2 * SPAN), F32),
             pltpu.VMEM((3, 8 * KR, SPAN), F32),
-            pltpu.VMEM((8 * KR, SPAN), F32),
-            pltpu.VMEM((KP, 8 * SPAN), BF16),
-            pltpu.VMEM((8, KP, KP), BF16),
-            pltpu.VMEM((8, KP, KP), BF16),
+            pltpu.VMEM((8 * KP, SPAN), F32),
+            pltpu.VMEM((8 * SPAN, KP), BF16),
+            pltpu.VMEM((8, KP, 2 * KP), BF16),
             pltpu.VMEM((3, rows, SPAN), F32),
             pltpu.VMEM((3, rows, SPAN), F32),
             pltpu.VMEM((SX * SD, SPAN), F32),
@@ -510,8 +510,7 @@
             pltpu.VMEM((3, TILES, SPAN), F32),
             pltpu.VMEM((SPAN, SPAN), BF16),
             pltpu.VMEM((SPAN, SPAN), BF16),
-            pltpu.VMEM((KP, 3 * KP), BF16),
-            pltpu.VMEM((KP, 3 * KP), BF16),
+            pltpu.VMEM((KP, 6 * KP), BF16),
             pltpu.VMEM((SWEEPS, 2, 3, SD, SPAN), BF16),
             pltpu.VMEM((SWEEPS, 2, 3, SD, SPAN), BF16),
             pltpu.VMEM((SWEEPS, 2, 3, SX, SPAN), BF16),

time: 49.9 us -> 49.5 us (level)
  no operation moved by 1% of the time
where the time goes in v3:
time: 49.5 us; the launch traced here: 49.4 us
  Pallas kernels  48.8 us (99%)
  between operations  0.64 us (1%)
    pallas_call x1, Pallas kernels, per_device(): pl.pallas_call(kernel, out_shape=tuple((pltpu.VMEM(shape, F32) for shape...  46.5 us
    pallas_call x1, Pallas kernels, per_device(): pl.pallas_call(write_out, out_shape=tuple((jax.ShapeDtypeStruct(shape, F3...  2.23 us

profile of v3, /device:TPU:1, one launch (start us, length us, event | category | flops | bytes accessed | tf_op | source)
XLA Modules:
  0.0 49.4 jit_solution(14988397416680758251)
XLA Ops:
  0.6 46.5 %shard_map.166 = (f32[3,3072,128]{2,1,0:T(8,128)S(1)}, f32[64,289]{1,0:T(8,128)S(1)}, f32[19,289]{1,0:T(8,128)S(1)}) custom-call(s32[1,128]{1,0:T(1,128)} %bitcast.22, s32[8,8]{1,0:T(8,128)} %bitcast.20, s32[1,8]{1,0:T(1,128)} %bitcast.23, s32[2,8]{1,0:T(2,128)} %bitcast.21, s32[2,8]{1,0:T(2,128)} %coct_in.1, s32[1,8]{1,0:T(1,128)} %bitcast.24, ...), custom_call_target="tpu_custom_call" | custom-call | flops 100000000 | bytes 12000000 | tf_op jit(solution)/shard_map/pallas_call | solution.py:477
  47.2 2.2 %shard_map.167 = (f32[3,3072,128]{2,1,0:T(8,128)}, f32[64,289]{1,0:T(8,128)}, f32[19,289]{1,0:T(8,128)}) custom-call(f32[3,3072,128]{2,1,0:T(8,128)S(1)} %get-tuple-element.9.refs_0_, f32[64,289]{1,0:T(8,128)S(1)} %get-tuple-element.10.refs_1_, f32[19,289]{1,0:T(8,128)S(1)} %get-tuple-element.11.refs_2_), custom_call_target="tpu_custom_call" | custom-call | tf_op jit(solution)/shard_map/pallas_call | solution.py:559

commit v4 on v3

--- a/solution.py
+++ b/solution.py
@@ -420,6 +420,10 @@
     turn = order[:LEAVES, :LEAVES]
     leaves[...] = (dot(turn, h.astype(BF16)) + dot(turn, m.astype(BF16)) + dot(turn, l.astype(BF16)))[:, :COEF]
 
+    for n in range(SWEEPS):
+        halo_sent(n)
+    for copies in (meta1, meta2, data1, data2):
+        sent(copies)
     arrive(terms)
     halves = []
     for g in range(2):
@@ -440,6 +444,7 @@
     rows = along_stream(lambda p: e2s, e2r, e2ss, e2rs)
     start(rows)
     e2r[i] = e2s[...]
+    sent(terms)
     arrive(rows)
     total = e2r[0][:, 2 * KP :]
     for s in range(1, NS):
@@ -451,10 +456,7 @@
     for n in range(3):
         upper[pl.ds(2 * NS + n, 1), :] = total[:, n * KP : n * KP + COEF]
 
-    for n in range(SWEEPS):
-        halo_sent(n)
-    for copies in (meta1, meta2, data1, data2, terms, rows):
-        sent(copies)
+    sent(rows)
 
 
 def write_out(*refs):

time: 49.5 us -> 49.4 us (level)
  no operation moved by 1% of the time
where the time goes in v4:
time: 49.4 us; the launch traced here: 49.3 us
  Pallas kernels  48.6 us (98%)
  between operations  0.64 us (1%)
    pallas_call x1, Pallas kernels, per_device(): pl.pallas_call(kernel, out_shape=tuple((pltpu.VMEM(shape, F32) for shape...  46.4 us
    pallas_call x1, Pallas kernels, per_device(): pl.pallas_call(write_out, out_shape=tuple((jax.ShapeDtypeStruct(shape, F3...  2.23 us

profile of v4, /device:TPU:1, one launch (start us, length us, event | category | flops | bytes accessed | tf_op | source)
XLA Modules:
  0.0 49.3 jit_solution(6945774768306716800)
XLA Ops:
  0.6 46.4 %shard_map.166 = (f32[3,3072,128]{2,1,0:T(8,128)S(1)}, f32[64,289]{1,0:T(8,128)S(1)}, f32[19,289]{1,0:T(8,128)S(1)}) custom-call(s32[1,128]{1,0:T(1,128)} %bitcast.22, s32[8,8]{1,0:T(8,128)} %bitcast.20, s32[1,8]{1,0:T(1,128)} %bitcast.23, s32[2,8]{1,0:T(2,128)} %bitcast.21, s32[2,8]{1,0:T(2,128)} %coct_in.1, s32[1,8]{1,0:T(1,128)} %bitcast.24, ...), custom_call_target="tpu_custom_call" | custom-call | flops 100000000 | bytes 12000000 | tf_op jit(solution)/shard_map/pallas_call | solution.py:479
  47.0 2.2 %shard_map.167 = (f32[3,3072,128]{2,1,0:T(8,128)}, f32[64,289]{1,0:T(8,128)}, f32[19,289]{1,0:T(8,128)}) custom-call(f32[3,3072,128]{2,1,0:T(8,128)S(1)} %get-tuple-element.9.refs_0_, f32[64,289]{1,0:T(8,128)S(1)} %get-tuple-element.10.refs_1_, f32[19,289]{1,0:T(8,128)S(1)} %get-tuple-element.11.refs_2_), custom_call_target="tpu_custom_call" | custom-call | tf_op jit(solution)/shard_map/pallas_call | solution.py:561
